TPU v7x, 32 devices: a whole 2x2x4 slice. The times are simulated.
32 devices in a mesh: row: 16 (over z, y, x), rep: 2 (over core).
Axes of the slice: x: 2, y: 2, z: 4, core: 2. Of those that a mesh axis runs over, the one named last changes fastest.
Arguments:
- features: bfloat16 [8192, 256], P('row'), may hold values from -6 to 6
- weight: bfloat16 [256, 256], replicated, may hold values from -0.375 to 0.375
- bias: float32 [256], replicated, may hold values from -3 to 3
- cotangent: bfloat16 [8192, 256], P(('row', 'rep')), may hold values from -14 to 14
- tile_values: bfloat16 [16, 16, 8, 128, 128], P('row', 'rep'), may hold values from -0.125 to 0.125
- tile_index: int32 [16, 16, 8, 2], P('row', 'rep'), may hold values from 0 to 3
- tile_count: int32 [16, 16], P('row', 'rep'), may hold values from 0 to 8, as said below
- rev_values: bfloat16 [16, 16, 8, 128, 128], P('row', 'rep'), may hold values from -0.125 to 0.125
- rev_index: int32 [16, 16, 8, 2], P('row', 'rep'), may hold values from 0 to 3
- rev_count: int32 [16, 16], P('row', 'rep'), may hold values from 0 to 8, as said below
Outputs:
- activations: bfloat16 [8192, 256], P(('row', 'rep'))
- grad_features: bfloat16 [8192, 256], P(('row', 'rep'))
- grad_weight: float32 [256, 256], replicated
- grad_bias: float32 [256], replicated
Inputs may be any that keep to these rules, and one draw needn't show every extreme that they name: Slots t < tile_count[a, d] are used; some slab pair uses all 8 slots in every draw. Slots t < rev_count[a, d] are used; some slab pair uses all 8 slots in every draw.
All inputs are finite; a program needn't handle non-finite values.
Results may differ from a plain program's by a relative error of at most 0.006.
Values may be sent and summed in bfloat16 or wider, within the bound.
A program may use at most 64 MiB of HBM per device.

v0:
```python
import jax
import jax.numpy as jnp
from jax import lax
from jax.sharding import PartitionSpec as P

TILE = 128
BLOCKS = 4


def passed_along(value, axis, steps):
    count = lax.axis_size(axis)
    pairs = [(source, (source + steps) % count) for source in range(count)]
    return lax.ppermute(value, axis, pairs)


def section_term(current, tile_block, slot_index, counts):
    blocks = current.reshape(BLOCKS, TILE, current.shape[1])
    sources = jnp.take(blocks, slot_index[:, 1], axis=0)
    product = jnp.einsum("tab,tbf->taf", tile_block, sources, preferred_element_type=jnp.float32)
    usable = jnp.arange(slot_index.shape[0], dtype=jnp.int32) < counts
    placing = (
        (slot_index[:, 0][None, :] == jnp.arange(BLOCKS, dtype=jnp.int32)[:, None])
        & usable[None, :]
    ).astype(jnp.float32)
    return jnp.einsum("nt,taf->naf", placing, product, precision=lax.Precision.HIGHEST)


def first_source(source, sections):
    rep_index = lax.axis_index("rep")
    groups = lax.axis_size("rep")
    current = source
    for shift_bit in range(groups.bit_length() - 1):
        shifted = passed_along(current, "row", -(sections << shift_bit))
        current = jnp.where(rep_index >> shift_bit & 1 == 1, shifted, current)
    return current


def apply_tiles(source, values, slot_index, counts):
    sections = values.shape[1]
    current = first_source(source, sections)
    summed_rows = jnp.zeros((BLOCKS, TILE, source.shape[1]), jnp.float32)
    for section in range(sections):
        if section > 0:
            current = passed_along(current, "row", -1)
        summed_rows = summed_rows + section_term(
            current, values[0, section], slot_index[0, section], counts[0, section]
        )
    return summed_rows.reshape(source.shape[0], source.shape[1])


def reduce_part(partial_rows):
    return lax.psum(partial_rows, "rep")


def own_rows(matrix):
    share_size = matrix.shape[0] // lax.axis_size("rep")
    return lax.dynamic_slice_in_dim(matrix, lax.axis_index("rep") * share_size, share_size, 0)


def activate(preact, cotangent):
    sigmoid_pre = jax.nn.sigmoid(preact)
    activations = (preact * sigmoid_pre).astype(jnp.bfloat16)
    grad_pre = (
        cotangent.astype(jnp.float32) * sigmoid_pre * (1.0 + preact * (1.0 - sigmoid_pre))
    ).astype(jnp.bfloat16)
    return (activations, grad_pre)


def local(
    features,
    weight,
    bias,
    cotangent,
    tile_values,
    tile_index,
    tile_count,
    rev_values,
    rev_index,
    rev_count,
):
    node_total = features.shape[0] * lax.axis_size("row")
    grad_scale = float(node_total) ** (-0.5)
    summed = reduce_part(apply_tiles(features, tile_values, tile_index, tile_count))
    mixed_all = summed.astype(jnp.bfloat16)
    preact_all = jnp.dot(mixed_all, weight, preferred_element_type=jnp.float32) + bias
    cotangent_all = lax.all_gather(cotangent, "rep", axis=0, tiled=True)
    activ_all, grad_all = activate(preact_all, cotangent_all)
    image = jnp.einsum("ng,fg->nf", grad_all, weight, preferred_element_type=jnp.float32).astype(
        jnp.bfloat16
    )
    mixed_rows = own_rows(mixed_all)
    grad_pre = own_rows(grad_all)
    activations = own_rows(activ_all)
    weight_term = jnp.einsum("nf,ng->fg", mixed_rows, grad_pre, preferred_element_type=jnp.float32)
    bias_term = jnp.sum(grad_pre.astype(jnp.float32), axis=0)
    grad_weight, grad_bias = lax.psum((weight_term, bias_term), ("row", "rep"))
    back_rows = reduce_part(apply_tiles(image, rev_values, rev_index, rev_count))
    back_rows = own_rows(back_rows)
    return (
        activations,
        back_rows.astype(jnp.bfloat16),
        grad_weight * grad_scale,
        grad_bias * grad_scale,
    )


def solution(mesh):
    placed = (
        P("row", None),
        P(),
        P(),
        P(("row", "rep"), None),
        P("row", "rep", None, None, None),
        P("row", "rep", None, None),
        P("row", "rep"),
        P("row", "rep", None, None, None),
        P("row", "rep", None, None),
        P("row", "rep"),
    )
    return jax.shard_map(
        local,
        mesh=mesh,
        in_specs=placed,
        out_specs=(P(("row", "rep"), None), P(("row", "rep"), None), P(), P()),
        check_vma=False,
    )
```

profile of v0, /device:TPU:0, one launch (start us, length us, event | category | flops | bytes accessed | tf_op | source)
XLA Modules:
  0.0 381.1 jit_solution(8210804947538525664)
XLA Ops:
  7.2 4.1 %collective-permute-start = (bf16[512,256]{1,0:T(8,128)(2,1)}, bf16[512,256]{1,0:T(8,128)(2,1)S(1)}, u32[]{:S(2)}, u32[]{:S(2)}) collective-permute-start(bf16[512,256]{1,0:T(8,128)(2,1)} %param.12), channel_id=1, source_target_pairs={{0,16},{2,18},{4,20},{6,22},{8,24},{10,26},{12,28},{14,30},{16,0},... | collective-permute-start | bytes 786440 | tf_op jit(solution)/shard_map/ppermute | solution.py:13
  23.6 1.6 fusion.216
  38.3 1.6 fusion.215
  52.1 3.5 all_gather.3
  57.3 3.3 collective-permute-start.1
  63.6 2.1 collective-permute-done.1
  68.1 6.1 %collective-permute-start.2 = (bf16[512,256]{1,0:T(8,128)(2,1)S(1)}, bf16[512,256]{1,0:T(8,128)(2,1)S(1)}, u32[]{:S(2)}, u32[]{:S(2)}) collective-permute-start(bf16[512,256]{1,0:T(8,128)(2,1)S(1)} %collective-permute-done.1), channel_id=1, source_target_pairs={{0,30},{2,0},{4,2},{6,4},{8,6},{10,8},{12,10},{14,12},{16,14},{18,... | collective-permute-start | bytes 786440 | tf_op jit(solution)/shard_map/ppermute | solution.py:13
  75.6 2.9 collective-permute-done.2
  79.2 1.4 fusion.44
  81.1 6.1 %collective-permute-start.3 = (bf16[512,256]{1,0:T(8,128)(2,1)S(1)}, bf16[512,256]{1,0:T(8,128)(2,1)S(1)}, u32[]{:S(2)}, u32[]{:S(2)}) collective-permute-start(bf16[512,256]{1,0:T(8,128)(2,1)S(1)} %copy-done.2), channel_id=1, source_target_pairs={{0,30},{2,0},{4,2},{6,4},{8,6},{10,8},{12,10},{14,12},{16,14},{18,... | collective-permute-start | bytes 786440 | tf_op jit(solution)/shard_map/ppermute | solution.py:13
  88.5 2.6 collective-permute-done.3
  91.9 1.4 fusion.42
  93.8 6.1 %collective-permute-start.4 = (bf16[512,256]{1,0:T(8,128)(2,1)S(1)}, bf16[512,256]{1,0:T(8,128)(2,1)S(1)}, u32[]{:S(2)}, u32[]{:S(2)}) collective-permute-start(bf16[512,256]{1,0:T(8,128)(2,1)S(1)} %copy-done.4), channel_id=1, source_target_pairs={{0,30},{2,0},{4,2},{6,4},{8,6},{10,8},{12,10},{14,12},{16,14},{18,... | collective-permute-start | bytes 786440 | tf_op jit(solution)/shard_map/ppermute | solution.py:13
  101.2 2.6 collective-permute-done.4
  104.6 1.4 fusion.40
  106.5 6.1 %collective-permute-start.5 = (bf16[512,256]{1,0:T(8,128)(2,1)S(1)}, bf16[512,256]{1,0:T(8,128)(2,1)S(1)}, u32[]{:S(2)}, u32[]{:S(2)}) collective-permute-start(bf16[512,256]{1,0:T(8,128)(2,1)S(1)} %copy-done.6), channel_id=1, source_target_pairs={{0,30},{2,0},{4,2},{6,4},{8,6},{10,8},{12,10},{14,12},{16,14},{18,... | collective-permute-start | bytes 786440 | tf_op jit(solution)/shard_map/ppermute | solution.py:13
  113.9 2.6 collective-permute-done.5
  117.2 1.4 fusion.38
  119.1 6.1 %collective-permute-start.6 = (bf16[512,256]{1,0:T(8,128)(2,1)S(1)}, bf16[512,256]{1,0:T(8,128)(2,1)S(1)}, u32[]{:S(2)}, u32[]{:S(2)}) collective-permute-start(bf16[512,256]{1,0:T(8,128)(2,1)S(1)} %copy-done.8), channel_id=1, source_target_pairs={{0,30},{2,0},{4,2},{6,4},{8,6},{10,8},{12,10},{14,12},{16,14},{18,... | collective-permute-start | bytes 786440 | tf_op jit(solution)/shard_map/ppermute | solution.py:13
  126.6 2.6 collective-permute-done.6
  129.9 1.4 fusion.36
  131.8 6.3 %collective-permute-start.7 = (bf16[512,256]{1,0:T(8,128)(2,1)S(1)}, bf16[512,256]{1,0:T(8,128)(2,1)S(1)}, u32[]{:S(2)}, u32[]{:S(2)}) collective-permute-start(bf16[512,256]{1,0:T(8,128)(2,1)S(1)} %copy-done.10), channel_id=1, source_target_pairs={{0,30},{2,0},{4,2},{6,4},{8,6},{10,8},{12,10},{14,12},{16,14},{18,... | collective-permute-start | bytes 786440 | tf_op jit(solution)/shard_map/ppermute | solution.py:13
  139.4 2.6 collective-permute-done.7
  142.7 1.4 fusion.34
  145.4 4.8 %all-reduce.5 = bf16[512,256]{1,0:T(8,128)(2,1)S(1)} all-reduce(f32[512,256]{1,0:T(8,128)S(1)} %bitcast.296), channel_id=1, replica_groups=mesh['row'=16,'rep'=2] {'rep'}, use_global_device_ids=true, to_apply=%region_0.2 | all-reduce | flops 131072 | bytes 786432 | tf_op jit(solution)/shard_map/psum | solution.py:52
  152.0 43.5 %psum.31 = f32[256]{0:T(256)S(1)} all-reduce(f32[256]{0:T(256)S(1)} %convert_reduce_fusion), channel_id=1, replica_groups=mesh['row'=16,'rep'=2] {'row','rep'}, use_global_device_ids=true, to_apply=%region_4.6 | all-reduce | flops 256 | bytes 2048 | tf_op jit(solution)/shard_map/psum | solution.py:96
  196.7 82.9 %all-reduce.4.cloned.1.call-done = f32[256,256]{1,0:T(8,128)} async-done(((f32[256,256]{1,0:T(8,128)}), f32[256,256]{1,0:T(8,128)}) %all-reduce.4.cloned.1.call-update) | async-done | bytes 262160 | tf_op jit(solution)/shard_map/psum | solution.py:96
  279.6 1.7 broadcast_multiply_fusion
  281.3 3.3 collective-permute-start.9
  287.9 1.5 collective-permute-done.9
  292.0 6.1 %collective-permute-start.10 = (bf16[512,256]{1,0:T(8,128)(2,1)S(1)}, bf16[512,256]{1,0:T(8,128)(2,1)S(1)}, u32[]{:S(2)}, u32[]{:S(2)}) collective-permute-start(bf16[512,256]{1,0:T(8,128)(2,1)S(1)} %collective-permute-done.9), channel_id=1, source_target_pairs={{0,30},{2,0},{4,2},{6,4},{8,6},{10,8},{12,10},{14,12},{16,14},{18,... | collective-permute-start | bytes 786440 | tf_op jit(solution)/shard_map/ppermute | solution.py:13
  299.4 2.6 collective-permute-done.10
  302.7 1.4 fusion.28
  304.7 6.1 %collective-permute-start.11 = (bf16[512,256]{1,0:T(8,128)(2,1)S(1)}, bf16[512,256]{1,0:T(8,128)(2,1)S(1)}, u32[]{:S(2)}, u32[]{:S(2)}) collective-permute-start(bf16[512,256]{1,0:T(8,128)(2,1)S(1)} %copy-done.12), channel_id=1, source_target_pairs={{0,30},{2,0},{4,2},{6,4},{8,6},{10,8},{12,10},{14,12},{16,14},{18,... | collective-permute-start | bytes 786440 | tf_op jit(solution)/shard_map/ppermute | solution.py:13
  312.1 2.6 collective-permute-done.11
  315.4 1.4 fusion.26
  317.3 6.1 %collective-permute-start.12 = (bf16[512,256]{1,0:T(8,128)(2,1)S(1)}, bf16[512,256]{1,0:T(8,128)(2,1)S(1)}, u32[]{:S(2)}, u32[]{:S(2)}) collective-permute-start(bf16[512,256]{1,0:T(8,128)(2,1)S(1)} %copy-done.14), channel_id=1, source_target_pairs={{0,30},{2,0},{4,2},{6,4},{8,6},{10,8},{12,10},{14,12},{16,14},{18,... | collective-permute-start | bytes 786440 | tf_op jit(solution)/shard_map/ppermute | solution.py:13
  324.7 2.6 collective-permute-done.12
  328.1 1.4 fusion.24
  330.0 6.4 %collective-permute-start.13 = (bf16[512,256]{1,0:T(8,128)(2,1)S(1)}, bf16[512,256]{1,0:T(8,128)(2,1)S(1)}, u32[]{:S(2)}, u32[]{:S(2)}) collective-permute-start(bf16[512,256]{1,0:T(8,128)(2,1)S(1)} %copy-done.16), channel_id=1, source_target_pairs={{0,30},{2,0},{4,2},{6,4},{8,6},{10,8},{12,10},{14,12},{16,14},{18,... | collective-permute-start | bytes 786440 | tf_op jit(solution)/shard_map/ppermute | solution.py:13
  337.5 2.7 collective-permute-done.13
  340.9 1.4 fusion.22
  342.8 6.1 %collective-permute-start.14 = (bf16[512,256]{1,0:T(8,128)(2,1)S(1)}, bf16[512,256]{1,0:T(8,128)(2,1)S(1)}, u32[]{:S(2)}, u32[]{:S(2)}) collective-permute-start(bf16[512,256]{1,0:T(8,128)(2,1)S(1)} %copy-done.18), channel_id=1, source_target_pairs={{0,30},{2,0},{4,2},{6,4},{8,6},{10,8},{12,10},{14,12},{16,14},{18,... | collective-permute-start | bytes 786440 | tf_op jit(solution)/shard_map/ppermute | solution.py:13
  349.6 3.3 collective-permute-done.14
  353.6 1.4 fusion.20
  355.5 6.1 %collective-permute-start.15 = (bf16[512,256]{1,0:T(8,128)(2,1)S(1)}, bf16[512,256]{1,0:T(8,128)(2,1)S(1)}, u32[]{:S(2)}, u32[]{:S(2)}) collective-permute-start(bf16[512,256]{1,0:T(8,128)(2,1)S(1)} %copy-done.20), channel_id=1, source_target_pairs={{0,30},{2,0},{4,2},{6,4},{8,6},{10,8},{12,10},{14,12},{16,14},{18,... | collective-permute-start | bytes 786440 | tf_op jit(solution)/shard_map/ppermute | solution.py:13
  362.3 3.3 collective-permute-done.15
  368.7 4.8 %all-reduce.6 = bf16[512,256]{1,0:T(8,128)(2,1)S(1)} all-reduce(f32[512,256]{1,0:T(8,128)S(1)} %bitcast.297), channel_id=1, replica_groups=mesh['row'=16,'rep'=2] {'rep'}, use_global_device_ids=true, to_apply=%region_1.3 | all-reduce | flops 131072 | bytes 786432 | tf_op jit(solution)/shard_map/psum | solution.py:52
  (201 shorter events, 84.8 us)
Async XLA Ops:
  7.2 143.1 %copy-start = (bf16[256,256]{1,0:T(8,128)(2,1)S(1)}, bf16[256,256]{1,0:T(8,128)(2,1)}, u32[]{:S(2)}) copy-start(bf16[256,256]{1,0:T(8,128)(2,1)} %param.13) | copy-start | bytes 393220
  7.2 272.4 %all-reduce.4.cloned.1.call-start = ((), (), s32[]{:S(2)}) async-start(), calls=%async_computation | async-start | bytes 524288 | tf_op jit(solution)/shard_map/psum | solution.py:96
  7.2 49.0 %collective-permute-start = (bf16[512,256]{1,0:T(8,128)(2,1)}, bf16[512,256]{1,0:T(8,128)(2,1)S(1)}, u32[]{:S(2)}, u32[]{:S(2)}) collective-permute-start(bf16[512,256]{1,0:T(8,128)(2,1)} %param.12), channel_id=1, source_target_pairs={{0,16},{2,18},{4,20},{6,22},{8,24},{10,26},{12,28},{14,30},{16,0},... | collective-permute-start | bytes 786440 | tf_op jit(solution)/shard_map/ppermute | solution.py:13
  57.3 8.4 %collective-permute-start.1 = (bf16[512,256]{1,0:T(8,128)(2,1)S(1)}, bf16[512,256]{1,0:T(8,128)(2,1)S(1)}, u32[]{:S(2)}, u32[]{:S(2)}) collective-permute-start(bf16[512,256]{1,0:T(8,128)(2,1)S(1)} %broadcast_select_fusion.1), channel_id=1, source_target_pairs={{0,30},{2,0},{4,2},{6,4},{8,6},{10,8},{12,10},{14,12},{16,14},{18,... | collective-permute-start | bytes 786440 | tf_op jit(solution)/shard_map/ppermute | solution.py:13
  68.1 10.4 %collective-permute-start.2 = (bf16[512,256]{1,0:T(8,128)(2,1)S(1)}, bf16[512,256]{1,0:T(8,128)(2,1)S(1)}, u32[]{:S(2)}, u32[]{:S(2)}) collective-permute-start(bf16[512,256]{1,0:T(8,128)(2,1)S(1)} %collective-permute-done.1), channel_id=1, source_target_pairs={{0,30},{2,0},{4,2},{6,4},{8,6},{10,8},{12,10},{14,12},{16,14},{18,... | collective-permute-start | bytes 786440 | tf_op jit(solution)/shard_map/ppermute | solution.py:13
  79.2 1.9 copy-start.2
  81.1 10.0 %collective-permute-start.3 = (bf16[512,256]{1,0:T(8,128)(2,1)S(1)}, bf16[512,256]{1,0:T(8,128)(2,1)S(1)}, u32[]{:S(2)}, u32[]{:S(2)}) collective-permute-start(bf16[512,256]{1,0:T(8,128)(2,1)S(1)} %copy-done.2), channel_id=1, source_target_pairs={{0,30},{2,0},{4,2},{6,4},{8,6},{10,8},{12,10},{14,12},{16,14},{18,... | collective-permute-start | bytes 786440 | tf_op jit(solution)/shard_map/ppermute | solution.py:13
  91.9 1.9 copy-start.4
  93.8 10.0 %collective-permute-start.4 = (bf16[512,256]{1,0:T(8,128)(2,1)S(1)}, bf16[512,256]{1,0:T(8,128)(2,1)S(1)}, u32[]{:S(2)}, u32[]{:S(2)}) collective-permute-start(bf16[512,256]{1,0:T(8,128)(2,1)S(1)} %copy-done.4), channel_id=1, source_target_pairs={{0,30},{2,0},{4,2},{6,4},{8,6},{10,8},{12,10},{14,12},{16,14},{18,... | collective-permute-start | bytes 786440 | tf_op jit(solution)/shard_map/ppermute | solution.py:13
  103.8 0.7 copy-start.5
  104.5 1.9 copy-start.6
  106.5 10.0 %collective-permute-start.5 = (bf16[512,256]{1,0:T(8,128)(2,1)S(1)}, bf16[512,256]{1,0:T(8,128)(2,1)S(1)}, u32[]{:S(2)}, u32[]{:S(2)}) collective-permute-start(bf16[512,256]{1,0:T(8,128)(2,1)S(1)} %copy-done.6), channel_id=1, source_target_pairs={{0,30},{2,0},{4,2},{6,4},{8,6},{10,8},{12,10},{14,12},{16,14},{18,... | collective-permute-start | bytes 786440 | tf_op jit(solution)/shard_map/ppermute | solution.py:13
  116.5 0.7 copy-start.7
  117.2 1.9 copy-start.8
  119.1 10.0 %collective-permute-start.6 = (bf16[512,256]{1,0:T(8,128)(2,1)S(1)}, bf16[512,256]{1,0:T(8,128)(2,1)S(1)}, u32[]{:S(2)}, u32[]{:S(2)}) collective-permute-start(bf16[512,256]{1,0:T(8,128)(2,1)S(1)} %copy-done.8), channel_id=1, source_target_pairs={{0,30},{2,0},{4,2},{6,4},{8,6},{10,8},{12,10},{14,12},{16,14},{18,... | collective-permute-start | bytes 786440 | tf_op jit(solution)/shard_map/ppermute | solution.py:13
  129.2 0.7 copy-start.9
  129.9 1.9 copy-start.10
  131.8 10.2 %collective-permute-start.7 = (bf16[512,256]{1,0:T(8,128)(2,1)S(1)}, bf16[512,256]{1,0:T(8,128)(2,1)S(1)}, u32[]{:S(2)}, u32[]{:S(2)}) collective-permute-start(bf16[512,256]{1,0:T(8,128)(2,1)S(1)} %copy-done.10), channel_id=1, source_target_pairs={{0,30},{2,0},{4,2},{6,4},{8,6},{10,8},{12,10},{14,12},{16,14},{18,... | collective-permute-start | bytes 786440 | tf_op jit(solution)/shard_map/ppermute | solution.py:13
  142.7 1.9 copy-start.27
  142.7 1.9 copy-start.35
  144.6 5.6 %copy-start.21 = (bf16[512,256]{1,0:T(8,128)(2,1)S(1)}, bf16[512,256]{1,0:T(8,128)(2,1)}, u32[]{:S(2)}) copy-start(bf16[512,256]{1,0:T(8,128)(2,1)} %all_gather.3) | copy-start | bytes 786436
  144.6 5.6 %copy-start.36 = (f32[256]{0:T(256)S(1)}, f32[256]{0:T(256)}, u32[]{:S(2)}) copy-start(f32[256]{0:T(256)} %param.14) | copy-start | bytes 3076
  150.9 134.5 %copy-start.33 = (pred[8]{0:T(512)(128)(4,1)S(1)}, pred[8]{0:T(512)(128)(4,1)}, u32[]{:S(2)}) copy-start(pred[8]{0:T(512)(128)(4,1)} %get-tuple-element.19) | copy-start | bytes 28
  151.9 129.4 %collective-permute-start.8 = (bf16[512,256]{1,0:T(8,128)(2,1)S(1)}, bf16[512,256]{1,0:T(8,128)(2,1)S(1)}, u32[]{:S(2)}, u32[]{:S(2)}) collective-permute-start(bf16[512,256]{1,0:T(8,128)(2,1)S(1)} %convolution_convert_fusion), channel_id=1, source_target_pairs={{0,16},{2,18},{4,20},{6,22},{8,24},{10,26},{12,28},{14,30},{16,0},... | collective-permute-start | bytes 786440 | tf_op jit(solution)/shard_map/ppermute | solution.py:13
  281.3 8.1 %collective-permute-start.9 = (bf16[512,256]{1,0:T(8,128)(2,1)S(1)}, bf16[512,256]{1,0:T(8,128)(2,1)S(1)}, u32[]{:S(2)}, u32[]{:S(2)}) collective-permute-start(bf16[512,256]{1,0:T(8,128)(2,1)S(1)} %broadcast_select_fusion), channel_id=1, source_target_pairs={{0,30},{2,0},{4,2},{6,4},{8,6},{10,8},{12,10},{14,12},{16,14},{18,... | collective-permute-start | bytes 786440 | tf_op jit(solution)/shard_map/ppermute | solution.py:13
  285.3 1.9 copy-start.22
  285.3 1.9 copy-start.28
  286.7 3.4 copy-start.31
  292.0 10.0 %collective-permute-start.10 = (bf16[512,256]{1,0:T(8,128)(2,1)S(1)}, bf16[512,256]{1,0:T(8,128)(2,1)S(1)}, u32[]{:S(2)}, u32[]{:S(2)}) collective-permute-start(bf16[512,256]{1,0:T(8,128)(2,1)S(1)} %collective-permute-done.9), channel_id=1, source_target_pairs={{0,30},{2,0},{4,2},{6,4},{8,6},{10,8},{12,10},{14,12},{16,14},{18,... | collective-permute-start | bytes 786440 | tf_op jit(solution)/shard_map/ppermute | solution.py:13
  302.0 0.7 copy-start.11
  302.7 1.9 copy-start.12
  304.7 10.0 %collective-permute-start.11 = (bf16[512,256]{1,0:T(8,128)(2,1)S(1)}, bf16[512,256]{1,0:T(8,128)(2,1)S(1)}, u32[]{:S(2)}, u32[]{:S(2)}) collective-permute-start(bf16[512,256]{1,0:T(8,128)(2,1)S(1)} %copy-done.12), channel_id=1, source_target_pairs={{0,30},{2,0},{4,2},{6,4},{8,6},{10,8},{12,10},{14,12},{16,14},{18,... | collective-permute-start | bytes 786440 | tf_op jit(solution)/shard_map/ppermute | solution.py:13
  315.4 1.9 copy-start.14
  317.3 10.0 %collective-permute-start.12 = (bf16[512,256]{1,0:T(8,128)(2,1)S(1)}, bf16[512,256]{1,0:T(8,128)(2,1)S(1)}, u32[]{:S(2)}, u32[]{:S(2)}) collective-permute-start(bf16[512,256]{1,0:T(8,128)(2,1)S(1)} %copy-done.14), channel_id=1, source_target_pairs={{0,30},{2,0},{4,2},{6,4},{8,6},{10,8},{12,10},{14,12},{16,14},{18,... | collective-permute-start | bytes 786440 | tf_op jit(solution)/shard_map/ppermute | solution.py:13
  328.1 8.3 %copy-start.24 = (s32[8]{0:T(128)S(1)}, s32[8]{0:T(128)}, u32[]{:S(2)}) copy-start(s32[8]{0:T(128)} %get-tuple-element.83) | copy-start | bytes 100
  328.1 1.9 copy-start.16
  330.0 10.2 %collective-permute-start.13 = (bf16[512,256]{1,0:T(8,128)(2,1)S(1)}, bf16[512,256]{1,0:T(8,128)(2,1)S(1)}, u32[]{:S(2)}, u32[]{:S(2)}) collective-permute-start(bf16[512,256]{1,0:T(8,128)(2,1)S(1)} %copy-done.16), channel_id=1, source_target_pairs={{0,30},{2,0},{4,2},{6,4},{8,6},{10,8},{12,10},{14,12},{16,14},{18,... | collective-permute-start | bytes 786440 | tf_op jit(solution)/shard_map/ppermute | solution.py:13
  340.9 8.1 %copy-start.23 = (s32[8]{0:T(128)S(1)}, s32[8]{0:T(128)}, u32[]{:S(2)}) copy-start(s32[8]{0:T(128)} %get-tuple-element.82) | copy-start | bytes 100
  340.9 8.1 %copy-start.34 = (pred[8]{0:T(512)(128)(4,1)S(1)}, pred[8]{0:T(512)(128)(4,1)}, u32[]{:S(2)}) copy-start(pred[8]{0:T(512)(128)(4,1)} %iota_compare_fusion.18) | copy-start | bytes 28
  340.9 1.9 copy-start.18
  342.8 10.0 %collective-permute-start.14 = (bf16[512,256]{1,0:T(8,128)(2,1)S(1)}, bf16[512,256]{1,0:T(8,128)(2,1)S(1)}, u32[]{:S(2)}, u32[]{:S(2)}) collective-permute-start(bf16[512,256]{1,0:T(8,128)(2,1)S(1)} %copy-done.18), channel_id=1, source_target_pairs={{0,30},{2,0},{4,2},{6,4},{8,6},{10,8},{12,10},{14,12},{16,14},{18,... | collective-permute-start | bytes 786440 | tf_op jit(solution)/shard_map/ppermute | solution.py:13
  353.6 8.1 %copy-start.26 = (s32[8]{0:T(128)S(1)}, s32[8]{0:T(128)}, u32[]{:S(2)}) copy-start(s32[8]{0:T(128)} %get-tuple-element.81) | copy-start | bytes 100
  353.6 8.1 %copy-start.32 = (pred[8]{0:T(512)(128)(4,1)S(1)}, pred[8]{0:T(512)(128)(4,1)}, u32[]{:S(2)}) copy-start(pred[8]{0:T(512)(128)(4,1)} %iota_compare_fusion.17) | copy-start | bytes 28
  353.6 1.9 copy-start.20
  355.5 10.6 %copy-start.30 = (pred[8]{0:T(512)(128)(4,1)S(1)}, pred[8]{0:T(512)(128)(4,1)}, u32[]{:S(2)}) copy-start(pred[8]{0:T(512)(128)(4,1)} %get-tuple-element.5) | copy-start | bytes 28
  355.5 10.0 %collective-permute-start.15 = (bf16[512,256]{1,0:T(8,128)(2,1)S(1)}, bf16[512,256]{1,0:T(8,128)(2,1)S(1)}, u32[]{:S(2)}, u32[]{:S(2)}) collective-permute-start(bf16[512,256]{1,0:T(8,128)(2,1)S(1)} %copy-done.20), channel_id=1, source_target_pairs={{0,30},{2,0},{4,2},{6,4},{8,6},{10,8},{12,10},{14,12},{16,14},{18,... | collective-permute-start | bytes 786440 | tf_op jit(solution)/shard_map/ppermute | solution.py:13
  366.1 1.9 copy-start.25
  366.1 1.9 copy-start.29
  (6 other events, 4.3 us)
Sparse Core Ops, SparseCore 0:
  152.1 127.4 all-reduce.3
where the time goes:
time: 382 us; the launch traced here: 381 us
  waiting for transfers between devices  119 us (31%)
  starting transfers between devices  84.8 us (22%)
  blocking collectives  56.7 us (15%)
  matrix products  40.4 us (11%)
  other arithmetic  35.9 us (9%)
  local copies, waits for them, and re-layouts  28.9 us (8%)
  between operations  15 us (4%)
    ppermute x16, starting transfers between devices, passed_along(): return lax.ppermute(value, axis, pairs)  84.7 us
    psum x1, waiting for transfers between devices, local(): grad_weight, grad_bias = lax.psum((weight_term, bias_term), ('row', 'rep'))  82.9 us
    psum x1, blocking collectives, local(): grad_weight, grad_bias = lax.psum((weight_term, bias_term), ('row', 'rep'))  43.5 us
    ppermute x16, waiting for transfers between devices, passed_along(): return lax.ppermute(value, axis, pairs)  36.6 us
    dot_general x16, matrix products, section_term(): jnp.einsum('tab,tbf->taf', tile_block, sources, preferred_element_type=jn...  22.4 us
    lt x16, other arithmetic, section_term(): usable = jnp.arange(slot_index.shape[0], dtype=jnp.int32) < counts  18.2 us
    dot_general x16, matrix products, section_term(): jnp.einsum('nt,taf->naf', placing, product, precision=lax.Precision.HIGHEST)  16.4 us
    gather x16, local copies, waits for them, and re-layouts, section_term(): sources = jnp.take(blocks, slot_index[:, 1], axis=0)  10.5 us
  transfers between devices with their start and end apart: 17, of which 15 were waited for; matrix products, arithmetic and copies ran while one was open for 17% of the time, Pallas kernels for 0%

commit v1 on v0

--- a/solution.py
+++ b/solution.py
@@ -49,7 +49,7 @@
 
 
 def reduce_part(partial_rows):
-    return lax.psum(partial_rows, "rep")
+    return jnp.sum(lax.all_gather(partial_rows, "rep"), axis=0)
 
 
 def own_rows(matrix):

time: 382 us -> 321 us (0.84)
  waiting for transfers between devices: 119 us -> 57.7 us
  blocking collectives: 56.7 us -> 42.5 us
  local copies, waits for them, and re-layouts: 28.9 us -> 35.8 us
  starting transfers between devices: 84.8 us -> 90.1 us
    psum x1, waiting for transfers between devices: 82.9 us -> 0.01 us  [local(): grad_weight, grad_bias = lax.psum((weight_term, bias_term), ('row', 'rep'))]
    ppermute x16, waiting for transfers between devices: 36.6 us -> 51.6 us  [passed_along(): return lax.ppermute(value, axis, pairs)]
    psum x2 -> x0, blocking collectives: 9.65 us -> none  [reduce_part(): return lax.psum(partial_rows, 'rep')]
    all_gather x0 -> x2, waiting for transfers between devices: none -> 6.11 us  [reduce_part(): return jnp.sum(lax.all_gather(partial_rows, 'rep'), axis=0)]
    gather x16, local copies, waits for them, and re-layouts: 10.5 us -> 16.2 us  [section_term(): sources = jnp.take(blocks, slot_index[:, 1], axis=0)]
    ppermute x16, starting transfers between devices: 84.7 us -> 90 us  [passed_along(): return lax.ppermute(value, axis, pairs)]
  transfers between devices with their start and end apart: 17 -> 19, of which waited for: 15 -> 16; matrix products, arithmetic and copies ran while one was open for 17% -> 28% of each run, Pallas kernels for 0% -> 0%
where the time goes in v1:
time: 321 us; the launch traced here: 320 us
  starting transfers between devices  90.1 us (28%)
  waiting for transfers between devices  57.7 us (18%)
  blocking collectives  42.5 us (13%)
  matrix products  39.7 us (12%)
  other arithmetic  39.2 us (12%)
  local copies, waits for them, and re-layouts  35.8 us (11%)
  between operations  14.9 us (5%)
    ppermute x16, starting transfers between devices, passed_along(): return lax.ppermute(value, axis, pairs)  90 us
    ppermute x16, waiting for transfers between devices, passed_along(): return lax.ppermute(value, axis, pairs)  51.6 us
    psum x1, blocking collectives, local(): grad_weight, grad_bias = lax.psum((weight_term, bias_term), ('row', 'rep'))  40.5 us
    dot_general x16, matrix products, section_term(): jnp.einsum('tab,tbf->taf', tile_block, sources, preferred_element_type=jn...  22.2 us
    lt x16, other arithmetic, section_term(): usable = jnp.arange(slot_index.shape[0], dtype=jnp.int32) < counts  18.2 us
    gather x16, local copies, waits for them, and re-layouts, section_term(): sources = jnp.take(blocks, slot_index[:, 1], axis=0)  16.2 us
    dot_general x16, matrix products, section_term(): jnp.einsum('nt,taf->naf', placing, product, precision=lax.Precision.HIGHEST)  15 us
    and x16, other arithmetic, section_term(): sources = jnp.take(blocks, slot_index[:, 1], axis=0)  8.41 us
  transfers between devices with their start and end apart: 19, of which 16 were waited for; matrix products, arithmetic and copies ran while one was open for 28% of the time, Pallas kernels for 0%

profile of v1, /device:TPU:0, one launch (start us, length us, event | category | flops | bytes accessed | tf_op | source)
XLA Modules:
  0.0 320.0 jit_solution(944693474219179211)
XLA Ops:
  7.2 4.1 %collective-permute-start = (bf16[512,256]{1,0:T(8,128)(2,1)}, bf16[512,256]{1,0:T(8,128)(2,1)S(1)}, u32[]{:S(2)}, u32[]{:S(2)}) collective-permute-start(bf16[512,256]{1,0:T(8,128)(2,1)} %param.12), channel_id=1, source_target_pairs={{0,16},{2,18},{4,20},{6,22},{8,24},{10,26},{12,28},{14,30},{16,0},... | collective-permute-start | bytes 786440 | tf_op jit(solution)/shard_map/ppermute | solution.py:13
  16.5 1.6 fusion.184
  33.7 1.6 fusion.183
  49.8 3.3 %collective-permute-start.1 = (bf16[512,256]{1,0:T(8,128)(2,1)S(1)}, bf16[512,256]{1,0:T(8,128)(2,1)S(1)}, u32[]{:S(2)}, u32[]{:S(2)}) collective-permute-start(bf16[512,256]{1,0:T(8,128)(2,1)S(1)} %broadcast_select_fusion.1), channel_id=1, source_target_pairs={{0,30},{2,0},{4,2},{6,4},{8,6},{10,8},{12,10},{14,12},{16,14},{18,... | collective-permute-start | bytes 786440 | tf_op jit(solution)/shard_map/ppermute | solution.py:13
  59.9 6.1 %collective-permute-start.2 = (bf16[512,256]{1,0:T(8,128)(2,1)S(1)}, bf16[512,256]{1,0:T(8,128)(2,1)S(1)}, u32[]{:S(2)}, u32[]{:S(2)}) collective-permute-start(bf16[512,256]{1,0:T(8,128)(2,1)S(1)} %collective-permute-done.1), channel_id=1, source_target_pairs={{0,30},{2,0},{4,2},{6,4},{8,6},{10,8},{12,10},{14,12},{16,14},{18,... | collective-permute-start | bytes 786440 | tf_op jit(solution)/shard_map/ppermute | solution.py:13
  67.3 2.6 collective-permute-done.2
  70.6 1.4 convolution_bitcast_fusion.13
  72.5 6.1 %collective-permute-start.3 = (bf16[512,256]{1,0:T(8,128)(2,1)S(1)}, bf16[512,256]{1,0:T(8,128)(2,1)S(1)}, u32[]{:S(2)}, u32[]{:S(2)}) collective-permute-start(bf16[512,256]{1,0:T(8,128)(2,1)S(1)} %copy-done.2), channel_id=1, source_target_pairs={{0,30},{2,0},{4,2},{6,4},{8,6},{10,8},{12,10},{14,12},{16,14},{18,... | collective-permute-start | bytes 786440 | tf_op jit(solution)/shard_map/ppermute | solution.py:13
  79.9 2.6 collective-permute-done.3
  83.3 1.4 convolution_bitcast_fusion.12
  85.2 6.1 %collective-permute-start.4 = (bf16[512,256]{1,0:T(8,128)(2,1)S(1)}, bf16[512,256]{1,0:T(8,128)(2,1)S(1)}, u32[]{:S(2)}, u32[]{:S(2)}) collective-permute-start(bf16[512,256]{1,0:T(8,128)(2,1)S(1)} %copy-done.4), channel_id=1, source_target_pairs={{0,30},{2,0},{4,2},{6,4},{8,6},{10,8},{12,10},{14,12},{16,14},{18,... | collective-permute-start | bytes 786440 | tf_op jit(solution)/shard_map/ppermute | solution.py:13
  92.6 2.6 collective-permute-done.4
  96.0 1.4 convolution_bitcast_fusion.11
  97.9 6.1 %collective-permute-start.5 = (bf16[512,256]{1,0:T(8,128)(2,1)S(1)}, bf16[512,256]{1,0:T(8,128)(2,1)S(1)}, u32[]{:S(2)}, u32[]{:S(2)}) collective-permute-start(bf16[512,256]{1,0:T(8,128)(2,1)S(1)} %copy-done.6), channel_id=1, source_target_pairs={{0,30},{2,0},{4,2},{6,4},{8,6},{10,8},{12,10},{14,12},{16,14},{18,... | collective-permute-start | bytes 786440 | tf_op jit(solution)/shard_map/ppermute | solution.py:13
  105.2 2.7 collective-permute-done.5
  108.6 1.4 convolution_bitcast_fusion.10
  110.5 6.1 %collective-permute-start.6 = (bf16[512,256]{1,0:T(8,128)(2,1)S(1)}, bf16[512,256]{1,0:T(8,128)(2,1)S(1)}, u32[]{:S(2)}, u32[]{:S(2)}) collective-permute-start(bf16[512,256]{1,0:T(8,128)(2,1)S(1)} %copy-done.8), channel_id=1, source_target_pairs={{0,30},{2,0},{4,2},{6,4},{8,6},{10,8},{12,10},{14,12},{16,14},{18,... | collective-permute-start | bytes 786440 | tf_op jit(solution)/shard_map/ppermute | solution.py:13
  118.0 2.6 collective-permute-done.6
  121.3 1.4 convolution_bitcast_fusion.9
  123.2 6.3 %collective-permute-start.7 = (bf16[512,256]{1,0:T(8,128)(2,1)S(1)}, bf16[512,256]{1,0:T(8,128)(2,1)S(1)}, u32[]{:S(2)}, u32[]{:S(2)}) collective-permute-start(bf16[512,256]{1,0:T(8,128)(2,1)S(1)} %copy-done.10), channel_id=1, source_target_pairs={{0,30},{2,0},{4,2},{6,4},{8,6},{10,8},{12,10},{14,12},{16,14},{18,... | collective-permute-start | bytes 786440 | tf_op jit(solution)/shard_map/ppermute | solution.py:13
  130.8 2.6 collective-permute-done.7
  137.8 2.0 all_gather.10
  142.6 6.1 %all-gather.3.cloned.1.call-done = f32[2,512,256]{2,1,0:T(8,128)} async-done(((f32[1,512,256]{2,1,0:T(8,128)}), f32[2,512,256]{2,1,0:T(8,128)}) %all-gather.3.cloned.1.call-update) | async-done | bytes 1048592 | tf_op jit(solution)/shard_map/all_gather | solution.py:52
  151.7 2.7 collective-permute-start.8
  157.1 9.9 %collective-permute-done.8 = bf16[512,256]{1,0:T(8,128)(2,1)S(1)} collective-permute-done((bf16[512,256]{1,0:T(8,128)(2,1)S(1)}, bf16[512,256]{1,0:T(8,128)(2,1)S(1)}, u32[]{:S(2)}, u32[]{:S(2)}) %collective-permute-start.8) | collective-permute-done | bytes 262176 | tf_op jit(solution)/shard_map/ppermute | solution.py:13
  167.0 5.5 %collective-permute-start.9 = (bf16[512,256]{1,0:T(8,128)(2,1)S(1)}, bf16[512,256]{1,0:T(8,128)(2,1)}, u32[]{:S(2)}, u32[]{:S(2)}) collective-permute-start(bf16[512,256]{1,0:T(8,128)(2,1)S(1)} %broadcast_select_fusion), channel_id=1, source_target_pairs={{0,30},{2,0},{4,2},{6,4},{8,6},{10,8},{12,10},{14,12},{16,14},{18,... | collective-permute-start | bytes 786440 | tf_op jit(solution)/shard_map/ppermute | solution.py:13
  175.8 2.9 collective-permute-done.9
  178.7 1.7 gather_fusion.9
  182.2 6.3 %collective-permute-start.10 = (bf16[512,256]{1,0:T(8,128)(2,1)}, bf16[512,256]{1,0:T(8,128)(2,1)}, u32[]{:S(2)}, u32[]{:S(2)}) collective-permute-start(bf16[512,256]{1,0:T(8,128)(2,1)} %collective-permute-done.9), channel_id=1, source_target_pairs={{0,30},{2,0},{4,2},{6,4},{8,6},{10,8},{12,10},{14,12},{16,14},{18,... | collective-permute-start | bytes 786440 | tf_op jit(solution)/shard_map/ppermute | solution.py:13
  189.8 4.2 %collective-permute-done.10 = bf16[512,256]{1,0:T(8,128)(2,1)} collective-permute-done((bf16[512,256]{1,0:T(8,128)(2,1)}, bf16[512,256]{1,0:T(8,128)(2,1)}, u32[]{:S(2)}, u32[]{:S(2)}) %collective-permute-start.10) | collective-permute-done | bytes 262176 | tf_op jit(solution)/shard_map/ppermute | solution.py:13
  194.0 1.5 gather_fusion.10
  195.5 1.4 convolution_bitcast_fusion.5
  197.4 6.2 %collective-permute-start.11 = (bf16[512,256]{1,0:T(8,128)(2,1)}, bf16[512,256]{1,0:T(8,128)(2,1)}, u32[]{:S(2)}, u32[]{:S(2)}) collective-permute-start(bf16[512,256]{1,0:T(8,128)(2,1)} %collective-permute-done.10), channel_id=1, source_target_pairs={{0,30},{2,0},{4,2},{6,4},{8,6},{10,8},{12,10},{14,12},{16,14},{18,... | collective-permute-start | bytes 786440 | tf_op jit(solution)/shard_map/ppermute | solution.py:13
  204.9 3.1 collective-permute-done.11
  208.0 1.5 gather_fusion.11
  211.4 6.3 %collective-permute-start.12 = (bf16[512,256]{1,0:T(8,128)(2,1)}, bf16[512,256]{1,0:T(8,128)(2,1)}, u32[]{:S(2)}, u32[]{:S(2)}) collective-permute-start(bf16[512,256]{1,0:T(8,128)(2,1)} %collective-permute-done.11), channel_id=1, source_target_pairs={{0,30},{2,0},{4,2},{6,4},{8,6},{10,8},{12,10},{14,12},{16,14},{18,... | collective-permute-start | bytes 786440 | tf_op jit(solution)/shard_map/ppermute | solution.py:13
  218.3 3.6 %collective-permute-done.12 = bf16[512,256]{1,0:T(8,128)(2,1)} collective-permute-done((bf16[512,256]{1,0:T(8,128)(2,1)}, bf16[512,256]{1,0:T(8,128)(2,1)}, u32[]{:S(2)}, u32[]{:S(2)}) %collective-permute-start.12) | collective-permute-done | bytes 262176 | tf_op jit(solution)/shard_map/ppermute | solution.py:13
  221.9 1.5 gather_fusion.12
  225.3 6.1 %collective-permute-start.13 = (bf16[512,256]{1,0:T(8,128)(2,1)}, bf16[512,256]{1,0:T(8,128)(2,1)}, u32[]{:S(2)}, u32[]{:S(2)}) collective-permute-start(bf16[512,256]{1,0:T(8,128)(2,1)} %collective-permute-done.12), channel_id=1, source_target_pairs={{0,30},{2,0},{4,2},{6,4},{8,6},{10,8},{12,10},{14,12},{16,14},{18,... | collective-permute-start | bytes 786440 | tf_op jit(solution)/shard_map/ppermute | solution.py:13
  232.0 3.6 %collective-permute-done.13 = bf16[512,256]{1,0:T(8,128)(2,1)} collective-permute-done((bf16[512,256]{1,0:T(8,128)(2,1)}, bf16[512,256]{1,0:T(8,128)(2,1)}, u32[]{:S(2)}, u32[]{:S(2)}) %collective-permute-start.13) | collective-permute-done | bytes 262176 | tf_op jit(solution)/shard_map/ppermute | solution.py:13
  235.6 1.5 gather_fusion.13
  239.1 6.4 %collective-permute-start.14 = (bf16[512,256]{1,0:T(8,128)(2,1)}, bf16[512,256]{1,0:T(8,128)(2,1)}, u32[]{:S(2)}, u32[]{:S(2)}) collective-permute-start(bf16[512,256]{1,0:T(8,128)(2,1)} %collective-permute-done.13), channel_id=1, source_target_pairs={{0,30},{2,0},{4,2},{6,4},{8,6},{10,8},{12,10},{14,12},{16,14},{18,... | collective-permute-start | bytes 786440 | tf_op jit(solution)/shard_map/ppermute | solution.py:13
  246.0 3.6 %collective-permute-done.14 = bf16[512,256]{1,0:T(8,128)(2,1)} collective-permute-done((bf16[512,256]{1,0:T(8,128)(2,1)}, bf16[512,256]{1,0:T(8,128)(2,1)}, u32[]{:S(2)}, u32[]{:S(2)}) %collective-permute-start.14) | collective-permute-done | bytes 262176 | tf_op jit(solution)/shard_map/ppermute | solution.py:13
  249.7 1.6 gather_fusion.14
  253.2 6.2 %collective-permute-start.15 = (bf16[512,256]{1,0:T(8,128)(2,1)}, bf16[512,256]{1,0:T(8,128)(2,1)S(1)}, u32[]{:S(2)}, u32[]{:S(2)}) collective-permute-start(bf16[512,256]{1,0:T(8,128)(2,1)} %collective-permute-done.14), channel_id=1, source_target_pairs={{0,30},{2,0},{4,2},{6,4},{8,6},{10,8},{12,10},{14,12},{16,14},{18,... | collective-permute-start | bytes 786440 | tf_op jit(solution)/shard_map/ppermute | solution.py:13
  260.0 3.7 %collective-permute-done.15 = bf16[512,256]{1,0:T(8,128)(2,1)S(1)} collective-permute-done((bf16[512,256]{1,0:T(8,128)(2,1)}, bf16[512,256]{1,0:T(8,128)(2,1)S(1)}, u32[]{:S(2)}, u32[]{:S(2)}) %collective-permute-start.15) | collective-permute-done | bytes 262176 | tf_op jit(solution)/shard_map/ppermute | solution.py:13
  268.0 40.5 %psum.15 = f32[256]{0:T(256)S(1)} all-reduce(f32[256]{0:T(256)S(1)} %convert_reduce_fusion), channel_id=1, replica_groups=mesh['row'=16,'rep'=2] {'row','rep'}, use_global_device_ids=true, to_apply=%region_4.6 | all-reduce | flops 256 | bytes 2048 | tf_op jit(solution)/shard_map/psum | solution.py:96
  309.8 1.7 broadcast_multiply_fusion
  (241 shorter events, 93.3 us)
Async XLA Ops:
  7.2 142.9 %copy-start = (bf16[256,256]{1,0:T(8,128)(2,1)S(1)}, bf16[256,256]{1,0:T(8,128)(2,1)}, u32[]{:S(2)}) copy-start(bf16[256,256]{1,0:T(8,128)(2,1)} %param.13) | copy-start | bytes 393220
  7.2 141.6 %all-gather.3.cloned.1.call-start = ((), (), s32[]{:S(2)}) async-start(), calls=%async_computation | async-start | bytes 1572864 | tf_op jit(solution)/shard_map/all_gather | solution.py:52
  7.2 41.6 %collective-permute-start = (bf16[512,256]{1,0:T(8,128)(2,1)}, bf16[512,256]{1,0:T(8,128)(2,1)S(1)}, u32[]{:S(2)}, u32[]{:S(2)}) collective-permute-start(bf16[512,256]{1,0:T(8,128)(2,1)} %param.12), channel_id=1, source_target_pairs={{0,16},{2,18},{4,20},{6,22},{8,24},{10,26},{12,28},{14,30},{16,0},... | collective-permute-start | bytes 786440 | tf_op jit(solution)/shard_map/ppermute | solution.py:13
  32.5 20.6 %copy-start.24 = (s32[8,2]{0,1:T(2,128)}, s32[8,2]{0,1:T(2,128)S(1)}, u32[]{:S(2)}) copy-start(s32[8,2]{0,1:T(2,128)S(1)} %get-tuple-element.43) | copy-start | bytes 196
  32.5 20.6 %copy-start.26 = (s32[8,2]{0,1:T(2,128)}, s32[8,2]{0,1:T(2,128)S(1)}, u32[]{:S(2)}) copy-start(s32[8,2]{0,1:T(2,128)S(1)} %get-tuple-element.44) | copy-start | bytes 196
  32.5 20.6 %copy-start.28 = (s32[8,2]{0,1:T(2,128)}, s32[8,2]{0,1:T(2,128)S(1)}, u32[]{:S(2)}) copy-start(s32[8,2]{0,1:T(2,128)S(1)} %get-tuple-element.45) | copy-start | bytes 196
  32.5 23.0 %copy-start.14 = (s32[8,2]{0,1:T(2,128)}, s32[8,2]{0,1:T(2,128)S(1)}, u32[]{:S(2)}) copy-start(s32[8,2]{0,1:T(2,128)S(1)} %get-tuple-element.39) | copy-start | bytes 196
  32.5 23.0 %copy-start.16 = (s32[8,2]{0,1:T(2,128)}, s32[8,2]{0,1:T(2,128)S(1)}, u32[]{:S(2)}) copy-start(s32[8,2]{0,1:T(2,128)S(1)} %get-tuple-element.46) | copy-start | bytes 196
  32.5 23.0 %copy-start.18 = (s32[8,2]{0,1:T(2,128)}, s32[8,2]{0,1:T(2,128)S(1)}, u32[]{:S(2)}) copy-start(s32[8,2]{0,1:T(2,128)S(1)} %get-tuple-element.40) | copy-start | bytes 196
  32.5 23.0 %copy-start.20 = (s32[8,2]{0,1:T(2,128)}, s32[8,2]{0,1:T(2,128)S(1)}, u32[]{:S(2)}) copy-start(s32[8,2]{0,1:T(2,128)S(1)} %get-tuple-element.41) | copy-start | bytes 196
  32.5 23.0 %copy-start.22 = (s32[8,2]{0,1:T(2,128)}, s32[8,2]{0,1:T(2,128)S(1)}, u32[]{:S(2)}) copy-start(s32[8,2]{0,1:T(2,128)S(1)} %get-tuple-element.42) | copy-start | bytes 196
  49.8 7.6 %collective-permute-start.1 = (bf16[512,256]{1,0:T(8,128)(2,1)S(1)}, bf16[512,256]{1,0:T(8,128)(2,1)S(1)}, u32[]{:S(2)}, u32[]{:S(2)}) collective-permute-start(bf16[512,256]{1,0:T(8,128)(2,1)S(1)} %broadcast_select_fusion.1), channel_id=1, source_target_pairs={{0,30},{2,0},{4,2},{6,4},{8,6},{10,8},{12,10},{14,12},{16,14},{18,... | collective-permute-start | bytes 786440 | tf_op jit(solution)/shard_map/ppermute | solution.py:13
  59.9 10.0 %collective-permute-start.2 = (bf16[512,256]{1,0:T(8,128)(2,1)S(1)}, bf16[512,256]{1,0:T(8,128)(2,1)S(1)}, u32[]{:S(2)}, u32[]{:S(2)}) collective-permute-start(bf16[512,256]{1,0:T(8,128)(2,1)S(1)} %collective-permute-done.1), channel_id=1, source_target_pairs={{0,30},{2,0},{4,2},{6,4},{8,6},{10,8},{12,10},{14,12},{16,14},{18,... | collective-permute-start | bytes 786440 | tf_op jit(solution)/shard_map/ppermute | solution.py:13
  72.5 10.0 %collective-permute-start.3 = (bf16[512,256]{1,0:T(8,128)(2,1)S(1)}, bf16[512,256]{1,0:T(8,128)(2,1)S(1)}, u32[]{:S(2)}, u32[]{:S(2)}) collective-permute-start(bf16[512,256]{1,0:T(8,128)(2,1)S(1)} %copy-done.2), channel_id=1, source_target_pairs={{0,30},{2,0},{4,2},{6,4},{8,6},{10,8},{12,10},{14,12},{16,14},{18,... | collective-permute-start | bytes 786440 | tf_op jit(solution)/shard_map/ppermute | solution.py:13
  85.2 10.0 %collective-permute-start.4 = (bf16[512,256]{1,0:T(8,128)(2,1)S(1)}, bf16[512,256]{1,0:T(8,128)(2,1)S(1)}, u32[]{:S(2)}, u32[]{:S(2)}) collective-permute-start(bf16[512,256]{1,0:T(8,128)(2,1)S(1)} %copy-done.4), channel_id=1, source_target_pairs={{0,30},{2,0},{4,2},{6,4},{8,6},{10,8},{12,10},{14,12},{16,14},{18,... | collective-permute-start | bytes 786440 | tf_op jit(solution)/shard_map/ppermute | solution.py:13
  97.9 10.0 %collective-permute-start.5 = (bf16[512,256]{1,0:T(8,128)(2,1)S(1)}, bf16[512,256]{1,0:T(8,128)(2,1)S(1)}, u32[]{:S(2)}, u32[]{:S(2)}) collective-permute-start(bf16[512,256]{1,0:T(8,128)(2,1)S(1)} %copy-done.6), channel_id=1, source_target_pairs={{0,30},{2,0},{4,2},{6,4},{8,6},{10,8},{12,10},{14,12},{16,14},{18,... | collective-permute-start | bytes 786440 | tf_op jit(solution)/shard_map/ppermute | solution.py:13
  110.5 10.0 %collective-permute-start.6 = (bf16[512,256]{1,0:T(8,128)(2,1)S(1)}, bf16[512,256]{1,0:T(8,128)(2,1)S(1)}, u32[]{:S(2)}, u32[]{:S(2)}) collective-permute-start(bf16[512,256]{1,0:T(8,128)(2,1)S(1)} %copy-done.8), channel_id=1, source_target_pairs={{0,30},{2,0},{4,2},{6,4},{8,6},{10,8},{12,10},{14,12},{16,14},{18,... | collective-permute-start | bytes 786440 | tf_op jit(solution)/shard_map/ppermute | solution.py:13
  123.2 10.9 %copy-start.50 = (pred[8]{0:T(512)(128)(4,1)S(1)}, pred[8]{0:T(512)(128)(4,1)}, u32[]{:S(2)}) copy-start(pred[8]{0:T(512)(128)(4,1)} %get-tuple-element.21) | copy-start | bytes 28
  123.2 10.2 %collective-permute-start.7 = (bf16[512,256]{1,0:T(8,128)(2,1)S(1)}, bf16[512,256]{1,0:T(8,128)(2,1)S(1)}, u32[]{:S(2)}, u32[]{:S(2)}) collective-permute-start(bf16[512,256]{1,0:T(8,128)(2,1)S(1)} %copy-done.10), channel_id=1, source_target_pairs={{0,30},{2,0},{4,2},{6,4},{8,6},{10,8},{12,10},{14,12},{16,14},{18,... | collective-permute-start | bytes 786440 | tf_op jit(solution)/shard_map/ppermute | solution.py:13
  136.1 6.0 %copy-start.15 = (s32[8,2]{0,1:T(2,128)S(1)}, s32[8,2]{0,1:T(2,128)}, u32[]{:S(2)}) copy-start(s32[8,2]{0,1:T(2,128)} %copy-done.14) | copy-start | bytes 196
  136.1 5.9 %copy-start.17 = (s32[8,2]{0,1:T(2,128)S(1)}, s32[8,2]{0,1:T(2,128)}, u32[]{:S(2)}) copy-start(s32[8,2]{0,1:T(2,128)} %copy-done.16) | copy-start | bytes 196
  136.8 13.3 %copy-start.53 = (f32[256]{0:T(256)S(1)}, f32[256]{0:T(256)}, u32[]{:S(2)}) copy-start(f32[256]{0:T(256)} %param.14) | copy-start | bytes 3076
  137.7 172.1 %all-reduce.2.cloned.1.call-start = ((), (), s32[]{:S(2)}) async-start(), calls=%async_computation.2 | async-start | bytes 524288 | tf_op jit(solution)/shard_map/psum | solution.py:96
  150.1 5.4 %copy-start.38 = (s32[8]{0:T(128)S(1)}, s32[8]{0:T(128)}, u32[]{:S(2)}) copy-start(s32[8]{0:T(128)} %get-tuple-element.6) | copy-start | bytes 100
  151.4 21.8 %copy-start.47 = (pred[8]{0:T(512)(128)(4,1)S(1)}, pred[8]{0:T(512)(128)(4,1)}, u32[]{:S(2)}) copy-start(pred[8]{0:T(512)(128)(4,1)} %get-tuple-element.19) | copy-start | bytes 28
  151.7 15.3 %collective-permute-start.8 = (bf16[512,256]{1,0:T(8,128)(2,1)S(1)}, bf16[512,256]{1,0:T(8,128)(2,1)S(1)}, u32[]{:S(2)}, u32[]{:S(2)}) collective-permute-start(bf16[512,256]{1,0:T(8,128)(2,1)S(1)} %convolution_convert_fusion), channel_id=1, source_target_pairs={{0,16},{2,18},{4,20},{6,22},{8,24},{10,26},{12,28},{14,30},{16,0},... | collective-permute-start | bytes 786440 | tf_op jit(solution)/shard_map/ppermute | solution.py:13
  157.1 154.4 %all-gather.5.cloned.1.call-start = ((), (), s32[]{:S(2)}) async-start(), calls=%async_computation.1 | async-start | bytes 1572864 | tf_op jit(solution)/shard_map/all_gather | solution.py:52
  167.0 11.6 %collective-permute-start.9 = (bf16[512,256]{1,0:T(8,128)(2,1)S(1)}, bf16[512,256]{1,0:T(8,128)(2,1)}, u32[]{:S(2)}, u32[]{:S(2)}) collective-permute-start(bf16[512,256]{1,0:T(8,128)(2,1)S(1)} %broadcast_select_fusion), channel_id=1, source_target_pairs={{0,30},{2,0},{4,2},{6,4},{8,6},{10,8},{12,10},{14,12},{16,14},{18,... | collective-permute-start | bytes 786440 | tf_op jit(solution)/shard_map/ppermute | solution.py:13
  182.2 11.8 %collective-permute-start.10 = (bf16[512,256]{1,0:T(8,128)(2,1)}, bf16[512,256]{1,0:T(8,128)(2,1)}, u32[]{:S(2)}, u32[]{:S(2)}) collective-permute-start(bf16[512,256]{1,0:T(8,128)(2,1)} %collective-permute-done.9), channel_id=1, source_target_pairs={{0,30},{2,0},{4,2},{6,4},{8,6},{10,8},{12,10},{14,12},{16,14},{18,... | collective-permute-start | bytes 786440 | tf_op jit(solution)/shard_map/ppermute | solution.py:13
  195.5 8.1 %copy-start.36 = (s32[8]{0:T(128)S(1)}, s32[8]{0:T(128)}, u32[]{:S(2)}) copy-start(s32[8]{0:T(128)} %get-tuple-element.85) | copy-start | bytes 100
  197.4 10.6 %collective-permute-start.11 = (bf16[512,256]{1,0:T(8,128)(2,1)}, bf16[512,256]{1,0:T(8,128)(2,1)}, u32[]{:S(2)}, u32[]{:S(2)}) collective-permute-start(bf16[512,256]{1,0:T(8,128)(2,1)} %collective-permute-done.10), channel_id=1, source_target_pairs={{0,30},{2,0},{4,2},{6,4},{8,6},{10,8},{12,10},{14,12},{16,14},{18,... | collective-permute-start | bytes 786440 | tf_op jit(solution)/shard_map/ppermute | solution.py:13
  209.5 8.2 %copy-start.35 = (s32[8]{0:T(128)S(1)}, s32[8]{0:T(128)}, u32[]{:S(2)}) copy-start(s32[8]{0:T(128)} %get-tuple-element.84) | copy-start | bytes 100
  209.5 8.2 %copy-start.46 = (pred[8]{0:T(512)(128)(4,1)S(1)}, pred[8]{0:T(512)(128)(4,1)}, u32[]{:S(2)}) copy-start(pred[8]{0:T(512)(128)(4,1)} %iota_compare_fusion.20) | copy-start | bytes 28
  211.4 10.5 %collective-permute-start.12 = (bf16[512,256]{1,0:T(8,128)(2,1)}, bf16[512,256]{1,0:T(8,128)(2,1)}, u32[]{:S(2)}, u32[]{:S(2)}) collective-permute-start(bf16[512,256]{1,0:T(8,128)(2,1)} %collective-permute-done.11), channel_id=1, source_target_pairs={{0,30},{2,0},{4,2},{6,4},{8,6},{10,8},{12,10},{14,12},{16,14},{18,... | collective-permute-start | bytes 786440 | tf_op jit(solution)/shard_map/ppermute | solution.py:13
  223.4 8.0 %copy-start.34 = (s32[8]{0:T(128)S(1)}, s32[8]{0:T(128)}, u32[]{:S(2)}) copy-start(s32[8]{0:T(128)} %get-tuple-element.83) | copy-start | bytes 100
  223.4 8.0 %copy-start.45 = (pred[8]{0:T(512)(128)(4,1)S(1)}, pred[8]{0:T(512)(128)(4,1)}, u32[]{:S(2)}) copy-start(pred[8]{0:T(512)(128)(4,1)} %iota_compare_fusion.19) | copy-start | bytes 28
  225.3 11.9 %copy-start.44 = (pred[8]{0:T(512)(128)(4,1)S(1)}, pred[8]{0:T(512)(128)(4,1)}, u32[]{:S(2)}) copy-start(pred[8]{0:T(512)(128)(4,1)} %get-tuple-element.9) | copy-start | bytes 28
  225.3 10.3 %collective-permute-start.13 = (bf16[512,256]{1,0:T(8,128)(2,1)}, bf16[512,256]{1,0:T(8,128)(2,1)}, u32[]{:S(2)}, u32[]{:S(2)}) collective-permute-start(bf16[512,256]{1,0:T(8,128)(2,1)} %collective-permute-done.12), channel_id=1, source_target_pairs={{0,30},{2,0},{4,2},{6,4},{8,6},{10,8},{12,10},{14,12},{16,14},{18,... | collective-permute-start | bytes 786440 | tf_op jit(solution)/shard_map/ppermute | solution.py:13
  237.2 8.3 %copy-start.32 = (s32[8]{0:T(128)S(1)}, s32[8]{0:T(128)}, u32[]{:S(2)}) copy-start(s32[8]{0:T(128)} %get-tuple-element.82) | copy-start | bytes 100
  237.2 8.2 %copy-start.43 = (pred[8]{0:T(512)(128)(4,1)S(1)}, pred[8]{0:T(512)(128)(4,1)}, u32[]{:S(2)}) copy-start(pred[8]{0:T(512)(128)(4,1)} %iota_compare_fusion.18) | copy-start | bytes 28
  239.1 12.3 %copy-start.42 = (pred[8]{0:T(512)(128)(4,1)S(1)}, pred[8]{0:T(512)(128)(4,1)}, u32[]{:S(2)}) copy-start(pred[8]{0:T(512)(128)(4,1)} %get-tuple-element.7) | copy-start | bytes 28
  239.1 10.6 %collective-permute-start.14 = (bf16[512,256]{1,0:T(8,128)(2,1)}, bf16[512,256]{1,0:T(8,128)(2,1)}, u32[]{:S(2)}, u32[]{:S(2)}) collective-permute-start(bf16[512,256]{1,0:T(8,128)(2,1)} %collective-permute-done.13), channel_id=1, source_target_pairs={{0,30},{2,0},{4,2},{6,4},{8,6},{10,8},{12,10},{14,12},{16,14},{18,... | collective-permute-start | bytes 786440 | tf_op jit(solution)/shard_map/ppermute | solution.py:13
  251.3 8.1 %copy-start.31 = (s32[8]{0:T(128)S(1)}, s32[8]{0:T(128)}, u32[]{:S(2)}) copy-start(s32[8]{0:T(128)} %get-tuple-element.81) | copy-start | bytes 100
  251.4 8.1 %copy-start.41 = (pred[8]{0:T(512)(128)(4,1)S(1)}, pred[8]{0:T(512)(128)(4,1)}, u32[]{:S(2)}) copy-start(pred[8]{0:T(512)(128)(4,1)} %iota_compare_fusion.17) | copy-start | bytes 28
  253.2 11.3 %copy-start.40 = (pred[8]{0:T(512)(128)(4,1)S(1)}, pred[8]{0:T(512)(128)(4,1)}, u32[]{:S(2)}) copy-start(pred[8]{0:T(512)(128)(4,1)} %get-tuple-element.5) | copy-start | bytes 28
  253.2 10.5 %collective-permute-start.15 = (bf16[512,256]{1,0:T(8,128)(2,1)}, bf16[512,256]{1,0:T(8,128)(2,1)S(1)}, u32[]{:S(2)}, u32[]{:S(2)}) collective-permute-start(bf16[512,256]{1,0:T(8,128)(2,1)} %collective-permute-done.14), channel_id=1, source_target_pairs={{0,30},{2,0},{4,2},{6,4},{8,6},{10,8},{12,10},{14,12},{16,14},{18,... | collective-permute-start | bytes 786440 | tf_op jit(solution)/shard_map/ppermute | solution.py:13
  266.4 42.2 %copy-start.12 = (f32[512,256]{1,0:T(8,128)S(1)}, f32[512,256]{1,0:T(8,128)}, u32[]{:S(2)}) copy-start(f32[512,256]{1,0:T(8,128)} %get-tuple-element.38) | copy-start | bytes 1572868
  266.4 42.1 %copy-start.13 = (f32[512,256]{1,0:T(8,128)S(1)}, f32[512,256]{1,0:T(8,128)}, u32[]{:S(2)}) copy-start(f32[512,256]{1,0:T(8,128)} %get-tuple-element.71) | copy-start | bytes 1572868
  (25 other events, 65.0 us)
Sparse Core Ops, SparseCore 0:
  137.8 10.8 all-gather.2
  157.2 124.5 all-reduce.1
  283.3 8.0 all-gather.4
